TPU v7x, 128 devices: a whole 4x4x4 slice. The times are simulated.
128 devices in a mesh: blk: 16 (over x, y), aux: 8 (over z, core).
Axes of the slice: x: 4, y: 4, z: 4, core: 2. Of those that a mesh axis runs over, the one named last changes fastest.
Arguments:
- factors: float32 [80, 256, 32, 256], P('blk', 'aux'), may hold values from -6 to 6
- partners: int32 [64, 10], replicated, may hold values from -1 to 63, as said below
- block_owner: int32 [64], replicated, may hold values from 0 to 15, as said below
Outputs:
- pair_blocks: float32 [80, 10, 256, 256], P('blk', None, 'aux')
- diag_blocks: float32 [80, 256, 256], P('blk', 'aux')
Inputs may be any that keep to these rules, and one draw needn't show every extreme that they name: `partners`: row a lists in increasing order the blocks c != a with |a - c| <= 5 that are significant with a, then -1 in the remaining slots; c is listed in row a exactly when a is listed in row c; some row lists 10 blocks. `block_owner`: never falls along the blocks; every index of blk holds 3 to 5 consecutive blocks, and some index holds exactly 5.
All inputs are finite; a program needn't handle non-finite values.
Results may differ from a plain program's by a relative error of at most 0.0003.
Values sent between devices are 32-bit elements; how exact they have to be, the bound alone decides.
A program may use at most 192 MiB of HBM per device.

v0:
```python
import functools
import math

import jax
import jax.numpy as jnp
import numpy as np
from jax import lax
from jax.experimental import pallas as pl
from jax.experimental.pallas import tpu as pltpu
from jax.sharding import PartitionSpec as P

MESH = pl.DeviceIdType.MESH
F32, BF16, I32 = jnp.float32, jnp.bfloat16, jnp.int32

SLOTS = 5
REACH = 5
RANKS = 8
ZDIM = 4
SHARD = 32

A1, A2, B1, B2, A3, B3 = 5, 6, 7, 8, 9, 10
FRONT, BACK = 16, 32


def _plan():
    own = [[(t, t + 1) for t in range(4)] + [(0, 0)]]
    own += [[(t, t + 2) for t in range(3)] + [(1, 1), (2, 2)]]
    own += [[(0, 3), (1, 4), (0, 4), (3, 3), (4, 4)]]
    first = [[(A1, BACK + s) for s in range(4)], [(B1, FRONT + t) for t in (1, 2, 3)]]
    second = [[(A2, BACK + 2), (A2, BACK + 3), (B2, FRONT + 1), (B2, FRONT + 2)]]
    second += [[(A1, BACK + 4), (B2, FRONT + 3), (B1, FRONT + 4)]]
    last = [[(A3, BACK + 2), (B3, FRONT + 2)]]
    return own + first + second + last


def _starts(sizes):
    return [sum(sizes[:g]) for g in range(len(sizes))]


PLAN = _plan()
GROUPS = len(PLAN)
LAST = GROUPS - 1
SIZES = [len(group) for group in PLAN]
OFFS = _starts(SIZES)
TOTAL = sum(SIZES)
AHEAD = [sum(key[0] in (A1, A2, A3) for key in group) for group in PLAN]
BEHIND = [sum(key[0] in (B1, B2, B3) for key in group) for group in PLAN]
RES_T = 36
RES_FA = [RES_T + 4 * GROUPS + start for start in _starts(AHEAD)]
RES_FB = [RES_FA[-1] + AHEAD[-1] + start for start in _starts(BEHIND)]
ZERO = RES_FB[-1] + BEHIND[-1]
NRES = ZERO + 1


def _tables():
    row, column, from_a, from_b = {}, {}, {}, {}
    for g, group in enumerate(PLAN):
        for i, key in enumerate(group):
            row[key] = OFFS[g] + i
            if i < 4:
                column[key] = RES_T + 4 * g + i
            if key[0] in (A1, A2, A3):
                from_a[key] = RES_FA[g] + i
            elif key[0] in (B1, B2, B3):
                from_b[key] = RES_FB[g] + i - AHEAD[g]
    table = np.full((3, SLOTS, 2 * REACH + 1, 2), ZERO, np.int32)
    aheads, behinds = (A1, A2, A3), (B1, B2, B3)
    for n in (3, 4, 5):
        for t in range(n):
            for d in range(1, REACH + 1):
                p = t + d
                if p < n:
                    places = [row[(t, p)]]
                else:
                    k, s = p - n + 1, n - 1 - t
                    places = []
                    if k <= 3 and (aheads[k - 1], BACK + s) in column:
                        places.append(column[(aheads[k - 1], BACK + s)])
                    if s <= 2 and (behinds[s], FRONT + k - 1) in from_b:
                        places.append(from_b[(behinds[s], FRONT + k - 1)])
                assert len(places) == (2 if p >= n and (k, s) == (3, 2) else 1), (n, t, d)
                table[n - 3, t, REACH + d, : len(places)] = places
                q = t - d
                if q >= 0:
                    places = [column[(q, t)]]
                else:
                    k = -q
                    places = []
                    if k <= 3 and (behinds[k - 1], FRONT + t) in column:
                        places.append(column[(behinds[k - 1], FRONT + t)])
                    if t <= 2 and (aheads[t], BACK + k - 1) in from_a:
                        places.append(from_a[(aheads[t], BACK + k - 1)])
                assert len(places) == (2 if q < 0 and (k, t) == (3, 2) else 1), (n, t, -d)
                table[n - 3, t, REACH - d, : len(places)] = places
    return np.concatenate([table.reshape(-1), [row[(t, t)] for t in range(SLOTS)]]).astype(np.int32)


TABLE = _tables()
NTAB = TABLE.shape[0]
DIAG = NTAB - SLOTS
LEFT = np.array([key[0] for group in PLAN for key in group], np.int32)
RIGHT = np.array([key[1] for group in PLAN for key in group], np.int32)
CONSTS = np.concatenate([TABLE, LEFT, RIGHT])


def kernel(
    blk_count,
    owner_hbm,
    partners_hbm,
    consts_hbm,
    fac_ref,
    pair_hbm,
    diag_hbm,
    owner_ref,
    partners_ref,
    consts_ref,
    pair_ref,
    diag_ref,
    head,
    own,
    staged,
    inbox,
    left_hi,
    left_lo,
    right_hi,
    right_lo,
    lthird_hi,
    lthird_lo,
    parts,
    from_core,
    out_across,
    out_up,
    out_down,
    relay_up,
    relay_down,
    sum_up,
    sum_down,
    rows_of,
    from_before,
    from_after,
    third,
    third_rows,
    third_up,
    third_down,
    third_relay,
    third_sums,
    third_own,
    t_out,
    t_in,
    res,
    right_at,
    place_at,
    scalar_sem,
    out_sem,
    head_sem,
    own_sem,
    y_send,
    y_recv,
    c_send,
    c_recv,
    z1_send,
    z1_recv,
    z2_send,
    z2_recv,
    t_send,
    t_recv,
    f_send,
    f_recv,
    l_send,
    l_recv,
):
    depth = own.shape[1]
    half = depth // 2
    blocks = owner_ref.shape[0]
    partner_slots = partners_ref.shape[0]
    scale = 1.0 / math.sqrt(RANKS * depth)

    b, r = lax.axis_index("blk"), lax.axis_index("aux")
    z, c = r // 2, r % 2
    after, before = (b + 1) % blk_count, (b + blk_count - 1) % blk_count
    up, down, across = (z + 1) % ZDIM, (z + 3) % ZDIM, (z + 2) % ZDIM
    dev_after, dev_before = (after, r), (before, r)
    dev_core = (b, 2 * z + 1 - c)
    dev_up, dev_down = (b, 2 * up + c), (b, 2 * down + c)

    owner_copy = pltpu.make_async_copy(owner_hbm, owner_ref, scalar_sem.at[0])
    owner_copy.start()
    partners_copy = pltpu.make_async_copy(partners_hbm, partners_ref, scalar_sem.at[1])
    consts_copy = pltpu.make_async_copy(consts_hbm, consts_ref, scalar_sem.at[2])
    head_copy = pltpu.make_async_copy(fac_ref.at[pl.ds(2, 3), pl.ds(0, half)], head, head_sem)
    head_copy.start()
    own_copies = [pltpu.make_async_copy(fac_ref.at[t], own.at[t], own_sem.at[t]) for t in range(SLOTS)]
    for t in (4, 3, 2, 1, 0):
        own_copies[t].start()

    barrier = pltpu.get_barrier_semaphore()
    peers = [(b, (r + k) % RANKS) for k in range(1, RANKS)] + [dev_after, dev_before]
    for peer in peers:
        pl.semaphore_signal(barrier, inc=1, device_id=peer, device_id_type=MESH)

    partners_copy.start()
    consts_copy.start()
    owner_copy.wait()

    def tally(i, carry):
        count, first = carry
        holder = owner_ref[i]
        return count + (holder == b).astype(I32), first + (holder < b).astype(I32)

    count, first = lax.fori_loop(0, blocks, tally, (jnp.int32(0), jnp.int32(0)))
    count = jnp.clip(count, 3, SLOTS)

    head_copy.wait()

    def stage_head(i, _):
        rows = pl.ds(pl.multiple_of(i * 64, 64), 64)
        staged[0][rows, :] = head[count - 3, rows, :]
        return 0

    lax.fori_loop(0, half // 64, stage_head, 0)
    pl.semaphore_wait(barrier, len(peers))

    def remote(src, dst, send, recv, device):
        return pltpu.make_async_remote_copy(
            src_ref=src, dst_ref=dst, send_sem=send, recv_sem=recv, device_id=device, device_id_type=MESH
        )

    chunks = [(k, half * i) for k in range(2) for i in range(2)]
    sends_a, sends_b = [], []
    for n, (k, start) in enumerate(chunks):
        rows = pl.ds(start, half)
        sends_a.append(remote(fac_ref.at[k, rows], inbox[k].at[rows], y_send.at[0, n], y_recv.at[0, n], dev_before))
        sends_b.append(
            remote(staged[k].at[rows], inbox[2 + k].at[rows], y_send.at[1, n], y_recv.at[1, n], dev_after)
        )

    third_a, third_b = [], []
    for n in range(2):
        rows, sems = pl.ds(half * n, half), (y_send.at[0, 4 + n], y_recv.at[0, 4 + n])
        third_a.append(remote(fac_ref.at[2, rows], third.at[rows], *sems, dev_before))
        third_b.append(remote(staged[2].at[rows], third.at[rows], *sems, dev_after))

    sends_a[0].start()
    sends_b[0].start()
    for n in range(1, len(chunks)):
        sends_a[n].start()

    @pl.when(c == 0)
    def _():
        for copy in third_a:
            copy.start()

    for t in (4, 3, 2, 1, 0):
        own_copies[t].wait()

    def stage(k, start):
        def move(i, _):
            rows = pl.ds(pl.multiple_of(start + i * 64, 64), 64)
            staged[k][rows, :] = own[count - 1 - k, rows, :]
            return 0

        lax.fori_loop(0, half // 64, move, 0)

    for n in range(1, len(chunks)):
        stage(*chunks[n])
        sends_b[n].start()

    @pl.when(c == 1)
    def _():
        for n in range(2):
            stage(2, half * n)
            third_b[n].start()

    def right_of(e, _):
        code = consts_ref[NTAB + TOTAL + e]
        s, t = code - BACK, code - FRONT
        from_back = jnp.where(s < count, count - 1 - s, B1 + s - count)
        from_front = jnp.where(t < count, t, A1 + t - count)
        right = jnp.where(code >= BACK, from_back, jnp.where(code >= FRONT, from_front, code))
        right_at[e] = jnp.clip(right, 0, B2)
        return 0


    def place_of(i, _):
        t, j = i // partner_slots, i % partner_slots
        a = jnp.clip(first + t, 0, blocks - 1)
        partner = partners_ref[j, a]
        d = jnp.clip(partner - a, -REACH, REACH)
        ok = (partner >= 0) & (t < count)
        at = (((count - 3) * SLOTS + t) * (2 * REACH + 1) + d + REACH) * 2
        at = jnp.clip(at, 0, DIAG - 2)
        place_at[2 * i] = jnp.where(ok, consts_ref[at], ZERO)
        place_at[2 * i + 1] = jnp.where(ok, consts_ref[at + 1], ZERO)
        return 0

    def look_up():
        lax.fori_loop(OFFS[3], TOTAL, right_of, 0)
        partners_copy.wait()
        lax.fori_loop(0, SLOTS * partner_slots, place_of, 0)
        res[ZERO] = jnp.zeros(res.shape[1:], F32)

    step = min(256, half)

    def split(x):
        hi = x.astype(BF16)
        return hi, (x - hi.astype(F32)).astype(BF16)

    def prepare(load, at, left=True, right=True):
        def body(i, _):
            rows = pl.ds(pl.multiple_of(i * step, step), step)
            x = load(rows)
            if right:
                right_hi[at, rows, :], right_lo[at, rows, :] = split(x)
            if left:
                left_hi[at, :, rows], left_lo[at, :, rows] = split(x.T)
            return 0

        lax.fori_loop(0, depth // step, body, 0)

    def prepare_third(n):
        def body(i, _):
            rows = pl.ds(pl.multiple_of(n * half + i * step, step), step)
            lthird_hi[:, rows], lthird_lo[:, rows] = split(third[rows, :].T)
            return 0

        lax.fori_loop(0, half // step, body, 0)

    def times(lh, ll, rh, rl):
        total = jnp.dot(lh, rh, preferred_element_type=F32)
        total += jnp.dot(lh, rl, preferred_element_type=F32)
        return total + jnp.dot(ll, rh, preferred_element_type=F32)

    def store(total, g, i):
        for rank in range(RANKS):
            parts[g][rank % 2, rank // 2, i] = total[rank * SHARD : (rank + 1) * SHARD]

    def over(g, body, start=0, stop=None):
        def run(i, _):
            body(i)
            return 0

        lax.fori_loop(start, SIZES[g] if stop is None else stop, run, 0)

    def products(g, start=0, stop=None):
        def body(i):
            left = jnp.clip(consts_ref[NTAB + OFFS[g] + i], 0, B2)
            right = jnp.clip(consts_ref[NTAB + TOTAL + i + OFFS[g]], 0, B2) if g < 3 else right_at[OFFS[g] + i]
            store(times(left_hi[left], left_lo[left], right_hi[right], right_lo[right]), g, i)

        over(g, body, start, stop)

    def product_third():
        right = jnp.where(c == 0, count - 3, 2)
        total = times(lthird_hi[...], lthird_lo[...], right_hi[right], right_lo[right])
        for rank in range(RANKS):
            third_rows[rank] = total[rank * SHARD : (rank + 1) * SHARD]
        for copy in third_relays():
            copy.start()

    def third_relays():
        return (
            remote(third_rows.at[2 * across], third_relay.at[0], z1_send.at[LAST, 0], z1_recv.at[LAST, 0], dev_up),
            remote(
                third_rows.at[2 * across + 1], third_relay.at[1], z1_send.at[LAST, 1], z1_recv.at[LAST, 1], dev_down
            ),
        )

    def third_copies():
        copies = [
            remote(third_rows.at[2 * z + 1 - c], third_own, l_send.at[4], l_recv.at[4], dev_core),
        ]
        for core in range(2):
            to_up, to_down = (b, 2 * up + core), (b, 2 * down + core)
            copies.append(remote(third_up.at[core], third_sums.at[c], l_send.at[core], l_recv.at[c], to_up))
            copies.append(
                remote(third_down.at[core], third_sums.at[2 + c], l_send.at[2 + core], l_recv.at[2 + c], to_down)
            )
        return copies

    def relay_third():
        for copy in third_relays():
            copy.wait_recv()
        third_up[0] = third_rows[2 * up] + third_relay[0]
        third_up[1] = third_rows[2 * up + 1]
        third_down[0] = third_rows[2 * down]
        third_down[1] = third_rows[2 * down + 1] + third_relay[1]
        for copy in third_copies():
            copy.start()

    def sum_third():
        remote(third_rows.at[0], third_own, l_send.at[4], l_recv.at[4], dev_core).wait_recv()
        for source in range(4):
            remote(third_rows.at[0], third_sums.at[source], l_send.at[0], l_recv.at[source], dev_core).wait_recv()
        kept, other = third_rows[2 * z + c], third_own[...]
        for source in range(2):
            total = jnp.where(c == source, kept, other) + (third_sums[source] + third_sums[2 + source])
            res[OFFS[LAST] + source] = total
            rows_of[LAST][source] = total

    def core_copy(g):
        return remote(parts[g].at[1 - c], from_core[g], c_send.at[g], c_recv.at[g], dev_core)

    def relay_copies(g):
        upper, lower = out_across[g].at[:, pl.ds(0, 16)], out_across[g].at[:, pl.ds(16, 16)]
        return (
            remote(upper, relay_up[g], z1_send.at[g, 0], z1_recv.at[g, 0], dev_up),
            remote(lower, relay_down[g], z1_send.at[g, 1], z1_recv.at[g, 1], dev_down),
        )

    def sum_copies(g):
        return (
            remote(out_up[g], sum_up[g], z2_send.at[g, 0], z2_recv.at[g, 0], dev_up),
            remote(out_down[g], sum_down[g], z2_send.at[g, 1], z2_recv.at[g, 1], dev_down),
        )

    def add_core(g):
        core_copy(g).wait_recv()

        def add_across(i):
            out_across[g][i] = parts[g][c, across, i] + from_core[g][across, i]

        over(g, add_across)
        for copy in relay_copies(g):
            copy.start()

    def add_relay(g):
        for copy in relay_copies(g):
            copy.wait_recv()

        def add(i):
            total = parts[g][c, up, i] + from_core[g][up, i]
            out_up[g][i, :16, :] = total[:16] + relay_up[g][i]
            out_up[g][i, 16:, :] = total[16:]
            total = parts[g][c, down, i] + from_core[g][down, i]
            out_down[g][i, :16, :] = total[:16]
            out_down[g][i, 16:, :] = total[16:] + relay_down[g][i]

        over(g, add)
        for copy in sum_copies(g):
            copy.start()

    def forward_copies(g):
        copies = []
        if AHEAD[g]:
            src = rows_of[g].at[pl.ds(0, AHEAD[g])]
            copies.append(remote(src, from_before[g], f_send.at[g, 0], f_recv.at[g, 0], dev_after))
        if BEHIND[g]:
            src = rows_of[g].at[pl.ds(AHEAD[g], BEHIND[g])]
            copies.append(remote(src, from_after[g], f_send.at[g, 1], f_recv.at[g, 1], dev_before))
        return copies

    def forward(g):
        for copy in forward_copies(g):
            copy.start()

    def turn_copy(g, k):
        to = (r + k) % RANKS
        return remote(t_out[g].at[to], t_in[g].at[r], t_send.at[g, k], t_recv.at[g, k], (b, to))

    def turn_arrival(g, k):
        to, source = (r + k) % RANKS, (r + RANKS - k) % RANKS
        return remote(t_out[g].at[to], t_in[g].at[source], t_send.at[g, k], t_recv.at[g, k], (b, to))

    def finish(g):
        for copy in sum_copies(g):
            copy.wait_recv()

        def add(i):
            total = (parts[g][c, z, i] + from_core[g][z, i]) + (sum_up[g][i] + sum_down[g][i])
            res[OFFS[g] + i] = total
            rows_of[g][i] = total

        over(g, add)
        turn(g)

    def turn(g):
        turned = res[OFFS[g] : OFFS[g] + 4].reshape(4 * SHARD, RANKS * SHARD).T
        for rank in range(RANKS):
            t_out[g][rank] = turned[rank * SHARD : (rank + 1) * SHARD]

        def send(k, _):
            turn_copy(g, k).start()
            return 0

        lax.fori_loop(1, RANKS, send, 0)

    def collect(g):
        def arrive(k, _):
            turn_arrival(g, k).wait_recv()
            return 0

        lax.fori_loop(1, RANKS, arrive, 0)
        t_in[g][r] = t_out[g][r]
        pieces = [t_in[g][rank] for rank in range(RANKS)]
        for i in range(min(4, SIZES[g])):
            lanes = slice(SHARD * i, SHARD * (i + 1))
            res[RES_T + 4 * g + i] = jnp.concatenate([piece[:, lanes] for piece in pieces], axis=1)

    def prepare_own(t, _):
        prepare(lambda rows: own[t, rows, :], t)
        return 0

    def receive(g):
        for copy in forward_copies(g):
            copy.wait_recv()
        for i in range(AHEAD[g]):
            res[RES_FA[g] + i] = from_before[g][i]
        for i in range(BEHIND[g]):
            res[RES_FB[g] + i] = from_after[g][i]

    def place(start, stop):
        def body(i, _):
            block = res[place_at[2 * i]] + res[place_at[2 * i + 1]]
            pair_ref[i // partner_slots, i % partner_slots] = block * scale
            return 0

        lax.fori_loop(start * partner_slots, stop * partner_slots, body, 0)

    def place_diag():
        def body(t, _):
            at = jnp.where(t < count, jnp.clip(consts_ref[DIAG + t], 0, ZERO), ZERO)
            diag_ref[t] = res[at] * scale
            return 0

        lax.fori_loop(0, SLOTS, body, 0)

    lax.fori_loop(0, SLOTS, prepare_own, 0)

    def arrived(*numbers):
        for n in numbers:
            sends_a[n].wait_recv()
            sends_b[n].wait_recv()

    def prepare_in(k, **sides):
        prepare(lambda rows: inbox[k][rows, :], A1 + k, **sides)
        prepare(lambda rows: inbox[2 + k][rows, :], B1 + k, **sides)

    def multiply(g):
        products(g)
        core_copy(g).start()

    consts_copy.wait()
    multiply(0)
    multiply(1)
    add_core(0)
    multiply(2)
    add_core(1)
    add_relay(0)
    add_core(2)
    add_relay(1)
    look_up()
    finish(0)
    add_relay(2)

    arrived(0, 1)
    prepare_in(0)
    multiply(3)
    finish(1)
    multiply(4)
    collect(0)
    add_core(3)
    finish(2)
    add_core(4)
    add_relay(3)
    collect(1)
    add_relay(4)
    collect(2)
    finish(3)
    finish(4)
    collect(3)
    collect(4)

    arrived(2, 3)
    prepare_in(1, right=False)
    multiply(5)
    prepare_in(1, left=False)
    products(6, 0, 2)
    add_core(5)
    products(6, 2, 3)
    core_copy(6).start()
    add_core(6)
    add_relay(5)
    third_a[0].wait_recv()
    prepare_third(0)

    third_a[1].wait_recv()
    prepare_third(1)
    product_third()
    add_relay(6)
    for g in (3, 4):
        forward(g)
    relay_third()
    finish(5)
    forward(5)
    finish(6)
    forward(6)
    sum_third()
    forward(LAST)
    turn(LAST)
    collect(5)
    collect(6)
    for g in (3, 4, 5, 6):
        receive(g)
    place(3, SLOTS)
    place_diag()
    out_copies = [pltpu.make_async_copy(pair_ref.at[t], pair_hbm.at[t], out_sem.at[t]) for t in range(SLOTS)]
    out_copies.append(pltpu.make_async_copy(diag_ref, diag_hbm, out_sem.at[SLOTS]))
    for t in range(3, SLOTS + 1):
        out_copies[t].start()
    collect(LAST)
    receive(LAST)
    place(0, 3)
    for t in range(3):
        out_copies[t].start()

    for copy in out_copies:
        copy.wait()
    for n in range(len(chunks)):
        sends_a[n].wait_send()
        sends_b[n].wait_send()
    for copy in (*third_a, *third_relays()):
        copy.wait_send()
    for copy in third_copies():
        copy.wait_send()
    for g in range(GROUPS):
        copies = forward_copies(g)
        if g < LAST:
            copies += [core_copy(g), *relay_copies(g), *sum_copies(g)]
        for copy in copies:
            copy.wait_send()

        def sent(k, _, g=g):
            turn_copy(g, k).wait_send()
            return 0

        lax.fori_loop(1, RANKS, sent, 0)


def deliver(pair_in, diag_in, pair_ref, diag_ref, pair_held, diag_held, in_sem, out_sem):
    slots = pair_in.shape[0]
    steps = [(pair_in.at[t], pair_held.at[t], pair_ref.at[t]) for t in range(slots)]
    steps.append((diag_in, diag_held, diag_ref))
    loads = [pltpu.make_async_copy(src, held, in_sem.at[i]) for i, (src, held, _) in enumerate(steps)]
    stores = [pltpu.make_async_copy(held, dst, out_sem.at[i]) for i, (_, held, dst) in enumerate(steps)]
    for load in loads:
        load.start()
    for load, store in zip(loads, stores):
        load.wait()
        store.start()
    for store in stores:
        store.wait()


def local(blk_count, factors, partners, block_owner):
    slots, aux_dev, occ, nb = factors.shape
    depth = aux_dev * occ
    half = depth // 2
    groups = GROUPS
    dma = pltpu.SemaphoreType.DMA
    hbm = pl.BlockSpec(memory_space=pl.ANY)

    def room(*shape):
        return pltpu.VMEM((*shape, nb), F32)

    def by_group(*lead, rows=SHARD, sizes=SIZES):
        return [room(*lead, size, rows) for size in sizes]

    found = pl.pallas_call(
        functools.partial(kernel, blk_count),
        out_shape=[
            jax.ShapeDtypeStruct((slots, partners.shape[1], SHARD, nb), F32),
            jax.ShapeDtypeStruct((slots, SHARD, nb), F32),
        ],
        in_specs=[hbm] * 4,
        out_specs=[hbm, hbm],
        scratch_shapes=[
            pltpu.SMEM(block_owner.shape, I32),
            pltpu.SMEM(partners.shape[::-1], I32),
            pltpu.SMEM(CONSTS.shape, I32),
            room(slots, partners.shape[1], SHARD),
            room(slots, SHARD),
            room(3, half),
            room(slots, depth),
            [room(depth)] * 3,
            [room(depth)] * 4,
            pltpu.VMEM((9, nb, depth), BF16),
            pltpu.VMEM((9, nb, depth), BF16),
            pltpu.VMEM((9, depth, nb), BF16),
            pltpu.VMEM((9, depth, nb), BF16),
            pltpu.VMEM((nb, depth), BF16),
            pltpu.VMEM((nb, depth), BF16),
            by_group(2, ZDIM, sizes=SIZES[:LAST]),
            by_group(ZDIM, sizes=SIZES[:LAST]),
            by_group(sizes=SIZES[:LAST]),
            by_group(sizes=SIZES[:LAST]),
            by_group(sizes=SIZES[:LAST]),
            by_group(rows=SHARD // 2, sizes=SIZES[:LAST]),
            by_group(rows=SHARD // 2, sizes=SIZES[:LAST]),
            by_group(sizes=SIZES[:LAST]),
            by_group(sizes=SIZES[:LAST]),
            by_group(),
            by_group(sizes=[max(1, size) for size in AHEAD]),
            by_group(sizes=[max(1, size) for size in BEHIND]),
            room(depth),
            room(RANKS, SHARD),
            room(2, SHARD),
            room(2, SHARD),
            room(2, SHARD),
            room(4, SHARD),
            room(SHARD),
            [pltpu.VMEM((RANKS, SHARD, 4 * SHARD), F32)] * GROUPS,
            [pltpu.VMEM((RANKS, SHARD, 4 * SHARD), F32)] * GROUPS,
            room(NRES, SHARD),
            pltpu.SMEM((TOTAL,), I32),
            pltpu.SMEM((2 * slots * partners.shape[1],), I32),
            dma((3,)),
            dma((slots + 1,)),
            dma,
            dma((SLOTS,)),
            dma((2, 6)),
            dma((2, 6)),
            dma((groups,)),
            dma((groups,)),
            dma((groups, 2)),
            dma((groups, 2)),
            dma((groups, 2)),
            dma((groups, 2)),
            dma((groups, RANKS)),
            dma((groups, RANKS)),
            dma((groups, 2)),
            dma((groups, 2)),
            dma((5,)),
            dma((5,)),
        ],
        compiler_params=pltpu.CompilerParams(
            collective_id=0, has_side_effects=True, vmem_limit_bytes=60 * 1024 * 1024
        ),
    )(block_owner, partners.T, jnp.asarray(CONSTS), factors.reshape(slots, depth, nb))
    return pl.pallas_call(
        deliver,
        out_shape=[jax.ShapeDtypeStruct(array.shape, array.dtype) for array in found],
        in_specs=[hbm, hbm],
        out_specs=[hbm, hbm],
        scratch_shapes=[*(pltpu.VMEM(array.shape, F32) for array in found), dma((slots + 1,)), dma((slots + 1,))],
    )(*found)


def solution(mesh):
    in_specs = (P("blk", "aux", None, None), P(), P())
    out_specs = (P("blk", None, "aux", None), P("blk", "aux", None))
    return jax.shard_map(
        functools.partial(local, mesh.shape["blk"]),
        mesh=mesh,
        in_specs=in_specs,
        out_specs=out_specs,
        check_vma=False,
    )
```

profile of v0, /device:TPU:1, one launch (start us, length us, event | category | flops | bytes accessed | tf_op | source)
XLA Modules:
  0.0 89.7 jit_solution(15099487297894091132)
XLA Ops:
  0.6 86.7 %shard_map.59 = (f32[5,10,32,256]{3,2,1,0:T(8,128)}, f32[5,32,256]{2,1,0:T(8,128)}) custom-call(s32[64]{0:T(128)} %owner_hbm.1, s32[10,64]{1,0:T(8,128)} %bitcast.3, s32[397]{0:T(512)} %constant.2.clone.consts_hbm, f32[5,1024,256]{2,1,0:T(8,128)} %bitcast.2), custom_call_target="tpu_custom_call" | custom-call | tf_op jit(solution)/shard_map/pallas_call | solution.py:668
  87.4 2.3 %shard_map.60 = (f32[5,10,32,256]{3,2,1,0:T(8,128)}, f32[5,32,256]{2,1,0:T(8,128)}) custom-call(f32[5,10,32,256]{3,2,1,0:T(8,128)} %get-tuple-element.4.pair_in, f32[5,32,256]{2,1,0:T(8,128)} %get-tuple-element.5.diag_in), custom_call_target="tpu_custom_call" | custom-call | tf_op jit(solution)/shard_map/pallas_call | solution.py:739
where the time goes:
time: 89.8 us; the launch traced here: 89.7 us
  Pallas kernels  89 us (99%)
    pallas_call x1, Pallas kernels, local(): pl.pallas_call(functools.partial(kernel, blk_count), out_shape=[jax.Shape...  86.7 us
    pallas_call x1, Pallas kernels, local(): pl.pallas_call(deliver, out_shape=[jax.ShapeDtypeStruct(array.shape, arra...  2.28 us

commit v1 on v0

--- a/solution.py
+++ b/solution.py
@@ -27,8 +27,8 @@
     own += [[(t, t + 2) for t in range(3)] + [(1, 1), (2, 2)]]
     own += [[(0, 3), (1, 4), (0, 4), (3, 3), (4, 4)]]
     first = [[(A1, BACK + s) for s in range(4)], [(B1, FRONT + t) for t in (1, 2, 3)]]
-    second = [[(A2, BACK + 2), (A2, BACK + 3), (B2, FRONT + 1), (B2, FRONT + 2)]]
-    second += [[(A1, BACK + 4), (B2, FRONT + 3), (B1, FRONT + 4)]]
+    second = [[(A2, BACK + 2), (A2, BACK + 3), (B2, FRONT + 2)]]
+    second += [[(A1, BACK + 4), (B2, FRONT + 1), (B2, FRONT + 3), (B1, FRONT + 4)]]
     last = [[(A3, BACK + 2), (B3, FRONT + 2)]]
     return own + first + second + last
 
@@ -305,7 +305,7 @@
         hi = x.astype(BF16)
         return hi, (x - hi.astype(F32)).astype(BF16)
 
-    def prepare(load, at, left=True, right=True):
+    def prepare(load, at, left=True, right=True, start=0, stop=depth):
         def body(i, _):
             rows = pl.ds(pl.multiple_of(i * step, step), step)
             x = load(rows)
@@ -315,7 +315,7 @@
                 left_hi[at, :, rows], left_lo[at, :, rows] = split(x.T)
             return 0
 
-        lax.fori_loop(0, depth // step, body, 0)
+        lax.fori_loop(start // step, stop // step, body, 0)
 
     def prepare_third(n):
         def body(i, _):
@@ -570,13 +570,15 @@
     collect(3)
     collect(4)
 
-    arrived(2, 3)
-    prepare_in(1, right=False)
+    arrived(2)
+    prepare_in(1, right=False, stop=half)
+    arrived(3)
+    prepare_in(1, right=False, start=half)
     multiply(5)
     prepare_in(1, left=False)
     products(6, 0, 2)
     add_core(5)
-    products(6, 2, 3)
+    products(6, 2, 4)
     core_copy(6).start()
     add_core(6)
     add_relay(5)

time: 89.8 us -> 88 us (0.980)
  Pallas kernels: 89 us -> 87.2 us
    pallas_call x1, Pallas kernels: 86.7 us -> 84.9 us  [local(): pl.pallas_call(functools.partial(kernel, blk_count), out_shape=[jax.Shape...]
where the time goes in v1:
time: 88 us; the launch traced here: 87.9 us
  Pallas kernels  87.2 us (99%)
    pallas_call x1, Pallas kernels, local(): pl.pallas_call(functools.partial(kernel, blk_count), out_shape=[jax.Shape...  84.9 us
    pallas_call x1, Pallas kernels, local(): pl.pallas_call(deliver, out_shape=[jax.ShapeDtypeStruct(array.shape, arra...  2.28 us

profile of v1, /device:TPU:1, one launch (start us, length us, event | category | flops | bytes accessed | tf_op | source)
XLA Modules:
  0.0 87.9 jit_solution(220515787042151059)
XLA Ops:
  0.6 84.9 %shard_map.59 = (f32[5,10,32,256]{3,2,1,0:T(8,128)}, f32[5,32,256]{2,1,0:T(8,128)}) custom-call(s32[64]{0:T(128)} %owner_hbm.1, s32[10,64]{1,0:T(8,128)} %bitcast.3, s32[397]{0:T(512)} %constant.2.clone.consts_hbm, f32[5,1024,256]{2,1,0:T(8,128)} %bitcast.2), custom_call_target="tpu_custom_call" | custom-call | tf_op jit(solution)/shard_map/pallas_call | solution.py:670
  85.6 2.3 %shard_map.60 = (f32[5,10,32,256]{3,2,1,0:T(8,128)}, f32[5,32,256]{2,1,0:T(8,128)}) custom-call(f32[5,10,32,256]{3,2,1,0:T(8,128)} %get-tuple-element.4.pair_in, f32[5,32,256]{2,1,0:T(8,128)} %get-tuple-element.5.diag_in), custom_call_target="tpu_custom_call" | custom-call | tf_op jit(solution)/shard_map/pallas_call | solution.py:741
